TPU v7x, 128 devices: a whole 4x4x4 slice. The times are simulated.
128 devices in a mesh: rows: 32 (over z, y, core), vecs: 4 (over x).
Axes of the slice: x: 4, y: 4, z: 4, core: 2. Of those that a mesh axis runs over, the one named last changes fastest.
Arguments:
- vectors: bfloat16 [131072, 1024], P('rows', 'vecs'), may hold values from -6 to 6, as said below
- blocks: bfloat16 [1024, 5, 128, 128], P('rows'), may hold values from -0.25 to 0.25
- columns: int32 [1024, 5], P('rows'), may hold values from 0 to 1023, as said below
Outputs:
- basis: float32 [131072, 1024], P('rows', 'vecs')
Inputs may be any that keep to these rules, and one draw needn't show every extreme that they name: Each block row i names 5 block columns of the form i + d clipped to 0 .. 1023, with distinct d in -8 .. 8; near the grid's ends some may repeat. `vectors`: entries of order one.
All inputs are finite; a program needn't handle non-finite values.
Results may differ from a plain program's by a relative error of at most 0.0075.
Values may be sent and summed in bfloat16 or wider, within the bound.
No kernel may reach another device: no remote copies, remote signals or barrier semaphores. Data moves between devices by JAX's collectives and lax.ppermute only.
A program may use at most 128 MiB of HBM per device.

v0:
```python
import jax
import jax.numpy as jnp
from jax import lax
from jax.sharding import PartitionSpec as P

DEGREE = 4
filter_center = 0.25
filter_radius = 1.25


def with_halo(shard, sides, width):
    for axis, dim in sides:
        count, length = (lax.axis_size(axis), shard.shape[dim])
        up = [(i, (i + 1) % count) for i in range(count - 1)]
        down = [(j, i) for i, j in up]
        last = lax.slice_in_dim(shard, length - width, length, axis=dim)
        first = lax.slice_in_dim(shard, 0, width, axis=dim)
        before = lax.ppermute(last, axis, up)
        after = lax.ppermute(first, axis, down)
        shard = jnp.concatenate([before, shard, after], axis=dim)
    return shard


def product(vec_bf, blocks, local_index):
    block_rows = blocks.shape[0]
    size_b = blocks.shape[2]
    width = vec_bf.shape[1]
    reach = block_rows // 4
    padded = with_halo(vec_bf, (("rows", 0),), reach * size_b)
    stacked = padded.reshape(block_rows + 2 * reach, size_b, width)
    picked = stacked[local_index]
    result = jnp.einsum("rjab,rjbk->rak", blocks, picked, preferred_element_type=jnp.float32)
    return result.reshape(block_rows * size_b, width)


def split_apply(left_bf, factor):
    factor_high = factor.astype(jnp.bfloat16)
    factor_low = (factor - factor_high.astype(jnp.float32)).astype(jnp.bfloat16)
    first = jnp.dot(left_bf, factor_high.T, preferred_element_type=jnp.float32)
    second = jnp.dot(left_bf, factor_low.T, preferred_element_type=jnp.float32)
    return first + second


def shards(vectors, blocks, columns):
    block_rows = blocks.shape[0]
    reach = block_rows // 4
    first_row = lax.axis_index("rows") * block_rows
    local_index = columns - first_row + reach
    total_rows = vectors.shape[0] * lax.axis_size("rows")
    older = vectors.astype(jnp.float32)
    current = (product(vectors, blocks, local_index) - filter_center * older) / filter_radius
    for iteration in range(1, DEGREE):
        rounded = current.astype(jnp.bfloat16)
        newer = (
            2.0 * (product(rounded, blocks, local_index) - filter_center * current) / filter_radius
            - older
        )
        older = current
        current = newer
    final = current.astype(jnp.bfloat16)
    panel_width = final.shape[1]
    full_width = panel_width * lax.axis_size("vecs")
    identity = jnp.eye(full_width, dtype=jnp.float32)
    whole_block = lax.all_gather(final, "vecs", axis=1, tiled=True)
    panel = jnp.dot(final.T, whole_block, preferred_element_type=jnp.float32)
    summed = lax.psum(panel, "rows")
    gram_matrix = lax.all_gather(summed, "vecs", axis=0, tiled=True) / total_rows
    lower = jnp.linalg.cholesky(gram_matrix)
    inverse = lax.linalg.triangular_solve(lower, identity, left_side=True, lower=True)
    own_rows = lax.dynamic_slice_in_dim(
        inverse, lax.axis_index("vecs") * panel_width, panel_width, 0
    )
    return split_apply(whole_block, own_rows)


def solution(mesh):
    in_specs = (P("rows", "vecs"), P("rows", None, None, None), P("rows", None))
    out_specs = P("rows", "vecs")
    return jax.shard_map(shards, mesh=mesh, in_specs=in_specs, out_specs=out_specs, check_vma=False)
```

profile of v0, /device:TPU:1, one launch (start us, length us, event | category | flops | bytes accessed | tf_op | source)
XLA Modules:
  0.0 772.8 jit_solution(1005979501189157616)
XLA Ops:
  25.1 7.6 gather_fusion
  32.7 7.5 fusion.88
  56.7 9.5 %gather_fusion.1 = bf16[160,128,256]{2,1,0:T(8,128)(2,1)} fusion(bf16[48,128,256]{2,1,0:T(8,128)(2,1)} %bitcast.194, s32[1024]{0:T(1024)S(1)} %pad_clamp_fusion), kind=kCustom, calls=%fused_computation.1 | custom fusion | bytes 20972160 | tf_op jit(solution)/shard_map/gather | solution.py:31
  66.2 7.5 fusion.89
  90.1 9.5 %gather_fusion.2 = bf16[160,128,256]{2,1,0:T(8,128)(2,1)} fusion(bf16[48,128,256]{2,1,0:T(8,128)(2,1)} %bitcast.195, s32[1024]{0:T(1024)S(1)} %pad_clamp_fusion), kind=kCustom, calls=%fused_computation.2 | custom fusion | bytes 20972160 | tf_op jit(solution)/shard_map/gather | solution.py:31
  99.6 7.5 fusion.90
  118.3 6.1 collective-permute-done.7
  126.3 9.5 %gather_fusion.3 = bf16[160,128,256]{2,1,0:T(8,128)(2,1)} fusion(bf16[48,128,256]{2,1,0:T(8,128)(2,1)} %bitcast.193, s32[1024]{0:T(1024)S(1)} %pad_clamp_fusion), kind=kCustom, calls=%fused_computation.3 | custom fusion | bytes 20972160 | tf_op jit(solution)/shard_map/gather | solution.py:31
  135.7 7.5 fusion.91
  149.4 94.6 %all-gather.3.cloned.1.call-done = bf16[4096,1024]{1,0:T(8,128)(2,1)} async-done(((bf16[4096,256]{1,0:T(8,128)(2,1)}), bf16[4096,1024]{1,0:T(8,128)(2,1)}) %all-gather.3.cloned.1.call-update) | async-done | bytes 8388624 | tf_op jit(solution)/shard_map/all_gather | solution.py:64
  244.0 8.4 %fusion.87 = f32[256,1024]{0,1:T(8,128)} fusion(bf16[4096,256]{1,0:T(8,128)(2,1)} %fusion.3, bf16[4096,1024]{1,0:T(8,128)(2,1)} %all-gather.3.cloned.1.call-done), kind=kOutput, calls=%fused_computation.195 | convolution fusion | flops 2147483648 | bytes 11534336 | tf_op jit(solution)/shard_map/dot_general | solution.py:65
  252.5 106.3 %all-reduce.3.cloned.1.call-done = f32[256,1024]{0,1:T(8,128)} async-done(((f32[256,1024]{0,1:T(8,128)}), f32[256,1024]{0,1:T(8,128)}) %all-reduce.3.cloned.1.call-update) | async-done | bytes 1048592 | tf_op jit(solution)/shard_map/psum | solution.py:66
  361.7 46.9 %all-gather.5.cloned.1.call-done = f32[1024,1024]{0,1:T(8,128)} async-done(((f32[256,1024]{0,1:T(8,128)}), f32[1024,1024]{0,1:T(8,128)}) %all-gather.5.cloned.1.call-update) | async-done | bytes 4194320 | tf_op jit(solution)/shard_map/all_gather | solution.py:67
  408.6 5.0 broadcast_multiply_fusion
  413.6 5.5 copy.8
  425.5 11.7 %cholesky.223 = f32[128,128]{1,0:T(8,128)S(1)} custom-call(f32[128,128]{1,0:T(8,128)S(1)} %cholesky.580), custom_call_target="Cholesky" | custom-call | tf_op jit(solution)/shard_map/jit(cholesky)/cholesky | solution.py:68
  437.3 9.8 %custom-call.62 = f32[1,128,128]{1,2,0:T(8,128)S(1)} custom-call(f32[1,128,128]{2,1,0:T(8,128)S(1)} %get-tuple-element.77), custom_call_target="InvertDiagBlocksLowerTriangular" | custom-call | tf_op jit(solution)/shard_map/jit(cholesky)/cholesky | solution.py:68
  453.5 11.9 %cholesky.244 = f32[128,128]{1,0:T(8,128)S(1)} custom-call(f32[128,128]{1,0:T(8,128)S(1)} %cholesky.584), custom_call_target="Cholesky" | custom-call | tf_op jit(solution)/shard_map/jit(cholesky)/cholesky | solution.py:68
  466.1 9.8 %custom-call.63 = f32[1,128,128]{1,2,0:T(8,128)S(1)} custom-call(f32[1,128,128]{2,1,0:T(8,128)S(1)} %get-tuple-element.74), custom_call_target="InvertDiagBlocksLowerTriangular" | custom-call | tf_op jit(solution)/shard_map/jit(cholesky)/cholesky | solution.py:68
  479.2 11.7 %cholesky.468 = f32[128,128]{1,0:T(8,128)S(1)} custom-call(f32[128,128]{1,0:T(8,128)S(1)} %cholesky.589), custom_call_target="Cholesky" | custom-call | tf_op jit(solution)/shard_map/jit(cholesky)/cholesky | solution.py:68
  492.2 9.8 %custom-call.64 = f32[1,128,128]{1,2,0:T(8,128)S(1)} custom-call(f32[1,128,128]{2,1,0:T(8,128)S(1)} %get-tuple-element.71), custom_call_target="InvertDiagBlocksLowerTriangular" | custom-call | tf_op jit(solution)/shard_map/jit(cholesky)/cholesky | solution.py:68
  505.5 12.1 %cholesky.487 = f32[128,128]{1,0:T(8,128)S(1)} custom-call(f32[128,128]{1,0:T(8,128)S(1)} %cholesky.594), custom_call_target="Cholesky" | custom-call | tf_op jit(solution)/shard_map/jit(cholesky)/cholesky | solution.py:68
  519.0 9.8 %custom-call.65 = f32[1,128,128]{1,2,0:T(8,128)S(1)} custom-call(f32[1,128,128]{2,1,0:T(8,128)S(1)} %get-tuple-element.68), custom_call_target="InvertDiagBlocksLowerTriangular" | custom-call | tf_op jit(solution)/shard_map/jit(cholesky)/cholesky | solution.py:68
  532.2 11.7 %cholesky.506 = f32[128,128]{1,0:T(8,128)S(1)} custom-call(f32[128,128]{1,0:T(8,128)S(1)} %cholesky.599), custom_call_target="Cholesky" | custom-call | tf_op jit(solution)/shard_map/jit(cholesky)/cholesky | solution.py:68
  545.2 10.0 %custom-call.66 = f32[1,128,128]{1,2,0:T(8,128)S(1)} custom-call(f32[1,128,128]{2,1,0:T(8,128)S(1)} %get-tuple-element.65), custom_call_target="InvertDiagBlocksLowerTriangular" | custom-call | tf_op jit(solution)/shard_map/jit(cholesky)/cholesky | solution.py:68
  558.5 11.7 %cholesky.526 = f32[128,128]{1,0:T(8,128)S(1)} custom-call(f32[128,128]{1,0:T(8,128)S(1)} %cholesky.604), custom_call_target="Cholesky" | custom-call | tf_op jit(solution)/shard_map/jit(cholesky)/cholesky | solution.py:68
  571.5 9.8 %custom-call.67 = f32[1,128,128]{1,2,0:T(8,128)S(1)} custom-call(f32[1,128,128]{2,1,0:T(8,128)S(1)} %get-tuple-element.62), custom_call_target="InvertDiagBlocksLowerTriangular" | custom-call | tf_op jit(solution)/shard_map/jit(cholesky)/cholesky | solution.py:68
  584.2 11.9 %cholesky.546 = f32[128,128]{1,0:T(8,128)S(1)} custom-call(f32[128,128]{1,0:T(8,128)S(1)} %cholesky.609), custom_call_target="Cholesky" | custom-call | tf_op jit(solution)/shard_map/jit(cholesky)/cholesky | solution.py:68
  597.5 9.8 %custom-call.68 = f32[1,128,128]{1,2,0:T(8,128)S(1)} custom-call(f32[1,128,128]{2,1,0:T(8,128)S(1)} %get-tuple-element.59), custom_call_target="InvertDiagBlocksLowerTriangular" | custom-call | tf_op jit(solution)/shard_map/jit(cholesky)/cholesky | solution.py:68
  609.9 11.7 %cholesky.564 = f32[128,128]{1,0:T(8,128)S(1)} custom-call(f32[128,128]{1,0:T(8,128)S(1)} %convolution_subtract_fusion.11), custom_call_target="Cholesky" | custom-call | tf_op jit(solution)/shard_map/jit(cholesky)/cholesky | solution.py:68
  633.4 23.9 %while.1 = (s32[]{:T(128)}, f32[1024,1024]{1,0:T(8,128)}, s32[8,2]{0,1:T(2,128)S(1)}, f32[8,128,128]{2,1,0:T(8,128)S(1)}, s32[]{:T(128)}) while((s32[]{:T(128)}, f32[1024,1024]{1,0:T(8,128)}, s32[8,2]{0,1:T(2,128)S(1)}, f32[8,128,128]{2,1,0:T(8,128)S(1)}, s32[]{:T(128)}) %tuple.61), condition=%wide.while_cond, body=%wide.while_body.sunk | while | flops 2 | bytes 131189 | solution.py:69
  657.3 79.0 %custom-call.69 = f32[8,128,128]{1,2,0:T(8,128)S(1)} custom-call(f32[8,128,128]{2,1,0:T(8,128)S(1)} %get-tuple-element.12), custom_call_target="InvertDiagBlocksLowerTriangular" | custom-call | tf_op jit(solution)/shard_map/triangular_solve | solution.py:69
  (153 shorter events, 172.5 us)
Async XLA Ops:
  6.5 237.5 %all-gather.3.cloned.1.call-start = ((), (), s32[]{:S(2)}) async-start(), calls=%async_computation | async-start | bytes 10485760 | tf_op jit(solution)/shard_map/all_gather | solution.py:64
  7.8 10.7 %collective-permute-start = (bf16[1024,256]{1,0:T(8,128)(2,1)S(1)}, bf16[1024,256]{1,0:T(8,128)(2,1)S(1)}, u32[]{:S(2)}, u32[]{:S(2)}) collective-permute-start(bf16[1024,256]{1,0:T(8,128)(2,1)S(1)} %get-tuple-element.29), channel_id=1, source_target_pairs={{0,4},{4,8},{8,12},{12,16},{16,20},{20,24},{24,28},{28,32},{32,36}... | collective-permute-start | bytes 1572872 | tf_op jit(solution)/shard_map/ppermute | solution.py:18
  12.4 10.6 %collective-permute-start.1 = (bf16[1024,256]{1,0:T(8,128)(2,1)S(1)}, bf16[1024,256]{1,0:T(8,128)(2,1)}, u32[]{:S(2)}, u32[]{:S(2)}) collective-permute-start(bf16[1024,256]{1,0:T(8,128)(2,1)S(1)} %get-tuple-element.30), channel_id=1, source_target_pairs={{4,0},{8,4},{12,8},{16,12},{20,16},{24,20},{28,24},{32,28},{36,32}... | collective-permute-start | bytes 1572872 | tf_op jit(solution)/shard_map/ppermute | solution.py:19
  18.5 0.8 copy-start.12
  32.7 7.5 copy-start.7
  40.3 2.0 copy-start
  42.4 8.0 %collective-permute-start.2 = (bf16[1024,256]{1,0:T(8,128)(2,1)S(1)}, bf16[1024,256]{1,0:T(8,128)(2,1)S(1)}, u32[]{:S(2)}, u32[]{:S(2)}) collective-permute-start(bf16[1024,256]{1,0:T(8,128)(2,1)S(1)} %get-tuple-element.27), channel_id=1, source_target_pairs={{0,4},{4,8},{8,12},{12,16},{16,20},{20,24},{24,28},{28,32},{32,36}... | collective-permute-start | bytes 1572872 | tf_op jit(solution)/shard_map/ppermute | solution.py:18
  44.3 10.5 %collective-permute-start.3 = (bf16[1024,256]{1,0:T(8,128)(2,1)S(1)}, bf16[1024,256]{1,0:T(8,128)(2,1)S(1)}, u32[]{:S(2)}, u32[]{:S(2)}) collective-permute-start(bf16[1024,256]{1,0:T(8,128)(2,1)S(1)} %get-tuple-element.28), channel_id=1, source_target_pairs={{4,0},{8,4},{12,8},{16,12},{20,16},{24,20},{28,24},{32,28},{36,32}... | collective-permute-start | bytes 1572872 | tf_op jit(solution)/shard_map/ppermute | solution.py:19
  66.2 7.5 copy-start.1
  73.7 2.1 copy-start.4
  75.9 8.0 %collective-permute-start.4 = (bf16[1024,256]{1,0:T(8,128)(2,1)S(1)}, bf16[1024,256]{1,0:T(8,128)(2,1)S(1)}, u32[]{:S(2)}, u32[]{:S(2)}) collective-permute-start(bf16[1024,256]{1,0:T(8,128)(2,1)S(1)} %get-tuple-element.25), channel_id=1, source_target_pairs={{0,4},{4,8},{8,12},{12,16},{16,20},{20,24},{24,28},{28,32},{32,36}... | collective-permute-start | bytes 1572872 | tf_op jit(solution)/shard_map/ppermute | solution.py:18
  77.8 10.5 %collective-permute-start.5 = (bf16[1024,256]{1,0:T(8,128)(2,1)S(1)}, bf16[1024,256]{1,0:T(8,128)(2,1)S(1)}, u32[]{:S(2)}, u32[]{:S(2)}) collective-permute-start(bf16[1024,256]{1,0:T(8,128)(2,1)S(1)} %get-tuple-element.26), channel_id=1, source_target_pairs={{4,0},{8,4},{12,8},{16,12},{20,16},{24,20},{28,24},{32,28},{36,32}... | collective-permute-start | bytes 1572872 | tf_op jit(solution)/shard_map/ppermute | solution.py:19
  99.6 7.5 copy-start.2
  99.6 8.0 %copy-start.5 = (f32[32,256,128,1]{1,2,3,0:T(8,128)S(1)}, f32[32,256,128,1]{1,2,3,0:T(8,128)}, u32[]{:S(2)}) copy-start(f32[32,256,128,1]{1,2,3,0:T(8,128)} %copy-done.4) | copy-start | bytes 12582916
  107.6 2.6 copy-start.8
  110.3 8.0 %collective-permute-start.6 = (bf16[1024,256]{1,0:T(8,128)(2,1)S(1)}, bf16[1024,256]{1,0:T(8,128)(2,1)S(1)}, u32[]{:S(2)}, u32[]{:S(2)}) collective-permute-start(bf16[1024,256]{1,0:T(8,128)(2,1)S(1)} %get-tuple-element.23), channel_id=1, source_target_pairs={{0,4},{4,8},{8,12},{12,16},{16,20},{20,24},{24,28},{28,32},{32,36}... | collective-permute-start | bytes 1572872 | tf_op jit(solution)/shard_map/ppermute | solution.py:18
  112.2 12.2 %collective-permute-start.7 = (bf16[1024,256]{1,0:T(8,128)(2,1)S(1)}, bf16[1024,256]{1,0:T(8,128)(2,1)S(1)}, u32[]{:S(2)}, u32[]{:S(2)}) collective-permute-start(bf16[1024,256]{1,0:T(8,128)(2,1)S(1)} %get-tuple-element.24), channel_id=1, source_target_pairs={{4,0},{8,4},{12,8},{16,12},{20,16},{24,20},{28,24},{32,28},{36,32}... | collective-permute-start | bytes 1572872 | tf_op jit(solution)/shard_map/ppermute | solution.py:19
  135.7 7.5 copy-start.3
  135.7 8.0 %copy-start.6 = (f32[32,256,128,1]{1,2,3,0:T(8,128)S(1)}, f32[32,256,128,1]{1,2,3,0:T(8,128)}, u32[]{:S(2)}) copy-start(f32[32,256,128,1]{1,2,3,0:T(8,128)} %copy-done.4) | copy-start | bytes 12582916
  135.7 9.2 %copy-start.9 = (f32[32,256,128,1]{1,2,3,0:T(8,128)S(1)}, f32[32,256,128,1]{1,2,3,0:T(8,128)}, u32[]{:S(2)}) copy-start(f32[32,256,128,1]{1,2,3,0:T(8,128)} %copy-done.8) | copy-start | bytes 12582916
  149.3 209.5 %all-reduce.3.cloned.1.call-start = ((), (), s32[]{:S(2)}) async-start(), calls=%async_computation.1 | async-start | bytes 2097152 | tf_op jit(solution)/shard_map/psum | solution.py:66
  252.5 156.1 %all-gather.5.cloned.1.call-start = ((), (), s32[]{:S(2)}) async-start(), calls=%async_computation.2 | async-start | bytes 5242880 | tf_op jit(solution)/shard_map/all_gather | solution.py:67
  423.6 1.9 copy-start.11
  736.3 3.2 copy-start.10
  747.7 11.2 %slice-start = ((s8[8388608]{0:T(1024)(128)(4,1)}), s8[4194304]{0:T(1024)(128)(4,1)S(1)}, s32[]{:S(2)}) async-start(s8[8388608]{0:T(1024)(128)(4,1)} %bitcast.197), calls=%async_computation.3 | async-start | bytes 8388608
  751.2 7.7 slice-start.1
Sparse Core Ops, SparseCore 0:
  149.5 94.5 all-gather.2
  252.6 106.2 all-reduce.2
  360.6 47.9 all-gather.4
where the time goes:
time: 782 us; the launch traced here: 773 us
  other arithmetic  287 us (37%)
  waiting for transfers between devices  280 us (36%)
  matrix products  91 us (12%)
  local copies, waits for them, and re-layouts  75.8 us (10%)
  starting transfers between devices  20.1 us (3%)
  between operations  18.8 us (2%)
    another operation x30, other arithmetic, shards(): lower = jnp.linalg.cholesky(gram_matrix)  172 us
    psum x1, waiting for transfers between devices, shards(): summed = lax.psum(panel, 'rows')  106 us
    all_gather x1, waiting for transfers between devices, shards(): whole_block = lax.all_gather(final, 'vecs', axis=1, tiled=True)  94.6 us
    another operation x3, other arithmetic, shards(): lax.linalg.triangular_solve(lower, identity, left_side=True, lower=True)  83.9 us
    all_gather x1, waiting for transfers between devices, shards(): lax.all_gather(summed, 'vecs', axis=0, tiled=True) / total_rows  46.9 us
    gather x4, local copies, waits for them, and re-layouts, product(): picked = stacked[local_index]  36.1 us
    dot_general x4, matrix products, product(): jnp.einsum('rjab,rjbk->rak', blocks, picked, preferred_element_type=jnp.f...  30.1 us
    another operation x24, local copies, waits for them, and re-layouts  23.8 us
  transfers between devices with their start and end apart: 11, of which 11 were waited for; matrix products, arithmetic and copies ran while one was open for 0% of the time, Pallas kernels for 0%

commit v1 on v0

--- a/solution.py
+++ b/solution.py
@@ -63,7 +63,8 @@
     identity = jnp.eye(full_width, dtype=jnp.float32)
     whole_block = lax.all_gather(final, "vecs", axis=1, tiled=True)
     panel = jnp.dot(final.T, whole_block, preferred_element_type=jnp.float32)
-    summed = lax.psum(panel, "rows")
+    pieces = lax.all_gather(panel, "rows")
+    summed = jnp.sum(pieces, axis=0)
     gram_matrix = lax.all_gather(summed, "vecs", axis=0, tiled=True) / total_rows
     lower = jnp.linalg.cholesky(gram_matrix)
     inverse = lax.linalg.triangular_solve(lower, identity, left_side=True, lower=True)

time: 782 us -> 800 us (1.023)
  other arithmetic: 287 us -> 299 us
    all_gather x0 -> x1, waiting for transfers between devices: none -> 116 us  [shards(): pieces = lax.all_gather(panel, 'rows')]
    psum x1 -> x0, waiting for transfers between devices: 106 us -> none  [shards(): summed = lax.psum(panel, 'rows')]
    reduce_sum x0 -> x1, other arithmetic: none -> 11.8 us  [shards(): summed = jnp.sum(pieces, axis=0)]
where the time goes in v1:
time: 800 us; the launch traced here: 791 us
  other arithmetic  299 us (37%)
  waiting for transfers between devices  287 us (36%)
  matrix products  89.9 us (11%)
  local copies, waits for them, and re-layouts  76.1 us (10%)
  starting transfers between devices  20.1 us (3%)
  between operations  19 us (2%)
    another operation x30, other arithmetic, shards(): lower = jnp.linalg.cholesky(gram_matrix)  173 us
    all_gather x1, waiting for transfers between devices, shards(): pieces = lax.all_gather(panel, 'rows')  116 us
    all_gather x1, waiting for transfers between devices, shards(): whole_block = lax.all_gather(final, 'vecs', axis=1, tiled=True)  94.6 us
    another operation x3, other arithmetic, shards(): lax.linalg.triangular_solve(lower, identity, left_side=True, lower=True)  83.9 us
    all_gather x1, waiting for transfers between devices, shards(): lax.all_gather(summed, 'vecs', axis=0, tiled=True) / total_rows  44.3 us
    gather x4, local copies, waits for them, and re-layouts, product(): picked = stacked[local_index]  36.1 us
    dot_general x4, matrix products, product(): jnp.einsum('rjab,rjbk->rak', blocks, picked, preferred_element_type=jnp.f...  30.1 us
    another operation x14, matrix products, shards(): lower = jnp.linalg.cholesky(gram_matrix)  22.9 us
  transfers between devices with their start and end apart: 11, of which 11 were waited for; matrix products, arithmetic and copies ran while one was open for 0% of the time, Pallas kernels for 0%

profile of v1, /device:TPU:1, one launch (start us, length us, event | category | flops | bytes accessed | tf_op | source)
XLA Modules:
  0.0 790.9 jit_solution(12371333019377978486)
XLA Ops:
  25.1 7.6 gather_fusion
  32.7 7.5 fusion.88
  56.7 9.5 %gather_fusion.1 = bf16[160,128,256]{2,1,0:T(8,128)(2,1)} fusion(bf16[48,128,256]{2,1,0:T(8,128)(2,1)} %bitcast.195, s32[1024]{0:T(1024)S(1)} %pad_clamp_fusion), kind=kCustom, calls=%fused_computation.1 | custom fusion | bytes 20972160 | tf_op jit(solution)/shard_map/gather | solution.py:31
  66.2 7.5 fusion.89
  90.1 9.5 %gather_fusion.2 = bf16[160,128,256]{2,1,0:T(8,128)(2,1)} fusion(bf16[48,128,256]{2,1,0:T(8,128)(2,1)} %bitcast.196, s32[1024]{0:T(1024)S(1)} %pad_clamp_fusion), kind=kCustom, calls=%fused_computation.2 | custom fusion | bytes 20972160 | tf_op jit(solution)/shard_map/gather | solution.py:31
  99.6 7.5 fusion.90
  118.3 6.1 collective-permute-done.7
  126.3 9.5 %gather_fusion.3 = bf16[160,128,256]{2,1,0:T(8,128)(2,1)} fusion(bf16[48,128,256]{2,1,0:T(8,128)(2,1)} %bitcast.194, s32[1024]{0:T(1024)S(1)} %pad_clamp_fusion), kind=kCustom, calls=%fused_computation.3 | custom fusion | bytes 20972160 | tf_op jit(solution)/shard_map/gather | solution.py:31
  135.7 7.5 fusion.91
  149.4 94.6 %all-gather.5.cloned.1.call-done = bf16[4096,1024]{1,0:T(8,128)(2,1)} async-done(((bf16[4096,256]{1,0:T(8,128)(2,1)}), bf16[4096,1024]{1,0:T(8,128)(2,1)}) %all-gather.5.cloned.1.call-update) | async-done | bytes 8388624 | tf_op jit(solution)/shard_map/all_gather | solution.py:64
  244.0 7.3 fusion.87
  251.4 115.8 %all-gather.9.cloned.1.call-done = f32[8192,1024]{1,0:T(8,128)} async-done(((f32[256,1024]{1,0:T(8,128)}), f32[8192,1024]{1,0:T(8,128)}) %all-gather.9.cloned.1.call-update) | async-done | bytes 33554448 | tf_op jit(solution)/shard_map/all_gather | solution.py:66
  367.2 11.8 %reduce_sum.9 = f32[256,1024]{1,0:T(8,128)S(1)} reduce(f32[32,256,1024]{2,1,0:T(8,128)} %bitcast.200, f32[]{:T(128)} %constant.301.clone.1), dimensions={0}, to_apply=%region_0.0 | reduce | flops 8126464 | bytes 34603012 | tf_op jit(solution)/shard_map/reduce_sum | solution.py:67
  383.2 44.3 %all-gather.7.cloned.1.call-done = f32[1024,1024]{0,1:T(8,128)} async-done(((f32[256,1024]{0,1:T(8,128)}), f32[1024,1024]{0,1:T(8,128)}) %all-gather.7.cloned.1.call-update) | async-done | bytes 4194320 | tf_op jit(solution)/shard_map/all_gather | solution.py:68
  432.6 5.5 copy.9
  444.6 11.7 %cholesky.223 = f32[128,128]{1,0:T(8,128)S(1)} custom-call(f32[128,128]{1,0:T(8,128)S(1)} %cholesky.580), custom_call_target="Cholesky" | custom-call | tf_op jit(solution)/shard_map/jit(cholesky)/cholesky | solution.py:69
  458.8 9.8 %custom-call.62 = f32[1,128,128]{1,2,0:T(8,128)S(1)} custom-call(f32[1,128,128]{2,1,0:T(8,128)S(1)} %get-tuple-element.77), custom_call_target="InvertDiagBlocksLowerTriangular" | custom-call | tf_op jit(solution)/shard_map/jit(cholesky)/cholesky | solution.py:69
  472.5 11.9 %cholesky.244 = f32[128,128]{1,0:T(8,128)S(1)} custom-call(f32[128,128]{1,0:T(8,128)S(1)} %cholesky.584), custom_call_target="Cholesky" | custom-call | tf_op jit(solution)/shard_map/jit(cholesky)/cholesky | solution.py:69
  485.1 9.8 %custom-call.63 = f32[1,128,128]{1,2,0:T(8,128)S(1)} custom-call(f32[1,128,128]{2,1,0:T(8,128)S(1)} %get-tuple-element.74), custom_call_target="InvertDiagBlocksLowerTriangular" | custom-call | tf_op jit(solution)/shard_map/jit(cholesky)/cholesky | solution.py:69
  498.2 11.7 %cholesky.468 = f32[128,128]{1,0:T(8,128)S(1)} custom-call(f32[128,128]{1,0:T(8,128)S(1)} %cholesky.589), custom_call_target="Cholesky" | custom-call | tf_op jit(solution)/shard_map/jit(cholesky)/cholesky | solution.py:69
  511.2 9.8 %custom-call.64 = f32[1,128,128]{1,2,0:T(8,128)S(1)} custom-call(f32[1,128,128]{2,1,0:T(8,128)S(1)} %get-tuple-element.71), custom_call_target="InvertDiagBlocksLowerTriangular" | custom-call | tf_op jit(solution)/shard_map/jit(cholesky)/cholesky | solution.py:69
  524.5 12.1 %cholesky.487 = f32[128,128]{1,0:T(8,128)S(1)} custom-call(f32[128,128]{1,0:T(8,128)S(1)} %cholesky.594), custom_call_target="Cholesky" | custom-call | tf_op jit(solution)/shard_map/jit(cholesky)/cholesky | solution.py:69
  538.0 9.8 %custom-call.65 = f32[1,128,128]{1,2,0:T(8,128)S(1)} custom-call(f32[1,128,128]{2,1,0:T(8,128)S(1)} %get-tuple-element.68), custom_call_target="InvertDiagBlocksLowerTriangular" | custom-call | tf_op jit(solution)/shard_map/jit(cholesky)/cholesky | solution.py:69
  551.2 11.7 %cholesky.506 = f32[128,128]{1,0:T(8,128)S(1)} custom-call(f32[128,128]{1,0:T(8,128)S(1)} %cholesky.599), custom_call_target="Cholesky" | custom-call | tf_op jit(solution)/shard_map/jit(cholesky)/cholesky | solution.py:69
  564.2 10.0 %custom-call.66 = f32[1,128,128]{1,2,0:T(8,128)S(1)} custom-call(f32[1,128,128]{2,1,0:T(8,128)S(1)} %get-tuple-element.65), custom_call_target="InvertDiagBlocksLowerTriangular" | custom-call | tf_op jit(solution)/shard_map/jit(cholesky)/cholesky | solution.py:69
  577.5 11.7 %cholesky.526 = f32[128,128]{1,0:T(8,128)S(1)} custom-call(f32[128,128]{1,0:T(8,128)S(1)} %cholesky.604), custom_call_target="Cholesky" | custom-call | tf_op jit(solution)/shard_map/jit(cholesky)/cholesky | solution.py:69
  590.5 9.8 %custom-call.67 = f32[1,128,128]{1,2,0:T(8,128)S(1)} custom-call(f32[1,128,128]{2,1,0:T(8,128)S(1)} %get-tuple-element.62), custom_call_target="InvertDiagBlocksLowerTriangular" | custom-call | tf_op jit(solution)/shard_map/jit(cholesky)/cholesky | solution.py:69
  603.3 11.9 %cholesky.546 = f32[128,128]{1,0:T(8,128)S(1)} custom-call(f32[128,128]{1,0:T(8,128)S(1)} %cholesky.609), custom_call_target="Cholesky" | custom-call | tf_op jit(solution)/shard_map/jit(cholesky)/cholesky | solution.py:69
  616.6 9.8 %custom-call.68 = f32[1,128,128]{1,2,0:T(8,128)S(1)} custom-call(f32[1,128,128]{2,1,0:T(8,128)S(1)} %get-tuple-element.59), custom_call_target="InvertDiagBlocksLowerTriangular" | custom-call | tf_op jit(solution)/shard_map/jit(cholesky)/cholesky | solution.py:69
  629.0 11.7 %cholesky.564 = f32[128,128]{1,0:T(8,128)S(1)} custom-call(f32[128,128]{1,0:T(8,128)S(1)} %convolution_subtract_fusion.11), custom_call_target="Cholesky" | custom-call | tf_op jit(solution)/shard_map/jit(cholesky)/cholesky | solution.py:69
  652.7 22.8 %while.1 = (s32[]{:T(128)}, f32[1024,1024]{1,0:T(8,128)}, s32[8,2]{0,1:T(2,128)S(1)}, f32[8,128,128]{2,1,0:T(8,128)S(1)}, s32[]{:T(128)}) while((s32[]{:T(128)}, f32[1024,1024]{1,0:T(8,128)}, s32[8,2]{0,1:T(2,128)S(1)}, f32[8,128,128]{2,1,0:T(8,128)S(1)}, s32[]{:T(128)}) %tuple.61), condition=%wide.while_cond, body=%wide.while_body.sunk | while | flops 2 | bytes 131181 | solution.py:70
  675.5 79.0 %custom-call.69 = f32[8,128,128]{1,2,0:T(8,128)S(1)} custom-call(f32[8,128,128]{2,1,0:T(8,128)S(1)} %get-tuple-element.12), custom_call_target="InvertDiagBlocksLowerTriangular" | custom-call | tf_op jit(solution)/shard_map/triangular_solve | solution.py:70
  (155 shorter events, 177.8 us)
Async XLA Ops:
  6.5 237.5 %all-gather.5.cloned.1.call-start = ((), (), s32[]{:S(2)}) async-start(), calls=%async_computation | async-start | bytes 10485760 | tf_op jit(solution)/shard_map/all_gather | solution.py:64
  7.8 10.7 %collective-permute-start = (bf16[1024,256]{1,0:T(8,128)(2,1)S(1)}, bf16[1024,256]{1,0:T(8,128)(2,1)S(1)}, u32[]{:S(2)}, u32[]{:S(2)}) collective-permute-start(bf16[1024,256]{1,0:T(8,128)(2,1)S(1)} %get-tuple-element.29), channel_id=1, source_target_pairs={{0,4},{4,8},{8,12},{12,16},{16,20},{20,24},{24,28},{28,32},{32,36}... | collective-permute-start | bytes 1572872 | tf_op jit(solution)/shard_map/ppermute | solution.py:18
  12.4 10.6 %collective-permute-start.1 = (bf16[1024,256]{1,0:T(8,128)(2,1)S(1)}, bf16[1024,256]{1,0:T(8,128)(2,1)}, u32[]{:S(2)}, u32[]{:S(2)}) collective-permute-start(bf16[1024,256]{1,0:T(8,128)(2,1)S(1)} %get-tuple-element.30), channel_id=1, source_target_pairs={{4,0},{8,4},{12,8},{16,12},{20,16},{24,20},{28,24},{32,28},{36,32}... | collective-permute-start | bytes 1572872 | tf_op jit(solution)/shard_map/ppermute | solution.py:19
  18.5 0.8 copy-start.12
  32.7 7.5 copy-start.7
  40.3 2.0 copy-start
  42.4 8.0 %collective-permute-start.2 = (bf16[1024,256]{1,0:T(8,128)(2,1)S(1)}, bf16[1024,256]{1,0:T(8,128)(2,1)S(1)}, u32[]{:S(2)}, u32[]{:S(2)}) collective-permute-start(bf16[1024,256]{1,0:T(8,128)(2,1)S(1)} %get-tuple-element.27), channel_id=1, source_target_pairs={{0,4},{4,8},{8,12},{12,16},{16,20},{20,24},{24,28},{28,32},{32,36}... | collective-permute-start | bytes 1572872 | tf_op jit(solution)/shard_map/ppermute | solution.py:18
  44.3 10.5 %collective-permute-start.3 = (bf16[1024,256]{1,0:T(8,128)(2,1)S(1)}, bf16[1024,256]{1,0:T(8,128)(2,1)S(1)}, u32[]{:S(2)}, u32[]{:S(2)}) collective-permute-start(bf16[1024,256]{1,0:T(8,128)(2,1)S(1)} %get-tuple-element.28), channel_id=1, source_target_pairs={{4,0},{8,4},{12,8},{16,12},{20,16},{24,20},{28,24},{32,28},{36,32}... | collective-permute-start | bytes 1572872 | tf_op jit(solution)/shard_map/ppermute | solution.py:19
  66.2 7.5 copy-start.1
  73.7 2.1 copy-start.4
  75.9 8.0 %collective-permute-start.4 = (bf16[1024,256]{1,0:T(8,128)(2,1)S(1)}, bf16[1024,256]{1,0:T(8,128)(2,1)S(1)}, u32[]{:S(2)}, u32[]{:S(2)}) collective-permute-start(bf16[1024,256]{1,0:T(8,128)(2,1)S(1)} %get-tuple-element.25), channel_id=1, source_target_pairs={{0,4},{4,8},{8,12},{12,16},{16,20},{20,24},{24,28},{28,32},{32,36}... | collective-permute-start | bytes 1572872 | tf_op jit(solution)/shard_map/ppermute | solution.py:18
  77.8 10.5 %collective-permute-start.5 = (bf16[1024,256]{1,0:T(8,128)(2,1)S(1)}, bf16[1024,256]{1,0:T(8,128)(2,1)S(1)}, u32[]{:S(2)}, u32[]{:S(2)}) collective-permute-start(bf16[1024,256]{1,0:T(8,128)(2,1)S(1)} %get-tuple-element.26), channel_id=1, source_target_pairs={{4,0},{8,4},{12,8},{16,12},{20,16},{24,20},{28,24},{32,28},{36,32}... | collective-permute-start | bytes 1572872 | tf_op jit(solution)/shard_map/ppermute | solution.py:19
  99.6 7.5 copy-start.2
  99.6 8.0 %copy-start.5 = (f32[32,256,128,1]{1,2,3,0:T(8,128)S(1)}, f32[32,256,128,1]{1,2,3,0:T(8,128)}, u32[]{:S(2)}) copy-start(f32[32,256,128,1]{1,2,3,0:T(8,128)} %copy-done.4) | copy-start | bytes 12582916
  107.6 2.6 copy-start.8
  110.3 8.0 %collective-permute-start.6 = (bf16[1024,256]{1,0:T(8,128)(2,1)S(1)}, bf16[1024,256]{1,0:T(8,128)(2,1)S(1)}, u32[]{:S(2)}, u32[]{:S(2)}) collective-permute-start(bf16[1024,256]{1,0:T(8,128)(2,1)S(1)} %get-tuple-element.23), channel_id=1, source_target_pairs={{0,4},{4,8},{8,12},{12,16},{16,20},{20,24},{24,28},{28,32},{32,36}... | collective-permute-start | bytes 1572872 | tf_op jit(solution)/shard_map/ppermute | solution.py:18
  112.2 12.2 %collective-permute-start.7 = (bf16[1024,256]{1,0:T(8,128)(2,1)S(1)}, bf16[1024,256]{1,0:T(8,128)(2,1)S(1)}, u32[]{:S(2)}, u32[]{:S(2)}) collective-permute-start(bf16[1024,256]{1,0:T(8,128)(2,1)S(1)} %get-tuple-element.24), channel_id=1, source_target_pairs={{4,0},{8,4},{12,8},{16,12},{20,16},{24,20},{28,24},{32,28},{36,32}... | collective-permute-start | bytes 1572872 | tf_op jit(solution)/shard_map/ppermute | solution.py:19
  135.7 7.5 copy-start.3
  135.7 8.0 %copy-start.6 = (f32[32,256,128,1]{1,2,3,0:T(8,128)S(1)}, f32[32,256,128,1]{1,2,3,0:T(8,128)}, u32[]{:S(2)}) copy-start(f32[32,256,128,1]{1,2,3,0:T(8,128)} %copy-done.4) | copy-start | bytes 12582916
  135.7 9.2 %copy-start.9 = (f32[32,256,128,1]{1,2,3,0:T(8,128)S(1)}, f32[32,256,128,1]{1,2,3,0:T(8,128)}, u32[]{:S(2)}) copy-start(f32[32,256,128,1]{1,2,3,0:T(8,128)} %copy-done.8) | copy-start | bytes 12582916
  149.3 217.9 %all-gather.9.cloned.1.call-start = ((), (), s32[]{:S(2)}) async-start(), calls=%async_computation.2 | async-start | bytes 34603008 | tf_op jit(solution)/shard_map/all_gather | solution.py:66
  251.4 176.2 %all-gather.7.cloned.1.call-start = ((), (), s32[]{:S(2)}) async-start(), calls=%async_computation.1 | async-start | bytes 5242880 | tf_op jit(solution)/shard_map/all_gather | solution.py:68
  442.6 2.0 copy-start.11
  754.5 3.2 copy-start.10
  765.9 11.2 %slice-start = ((s8[8388608]{0:T(1024)(128)(4,1)}), s8[4194304]{0:T(1024)(128)(4,1)S(1)}, s32[]{:S(2)}) async-start(s8[8388608]{0:T(1024)(128)(4,1)} %bitcast.198), calls=%async_computation.3 | async-start | bytes 8388608
  769.4 7.7 slice-start.1
Sparse Core Ops, SparseCore 0:
  149.5 94.5 all-gather.4
  251.5 115.6 all-gather.8
  380.5 46.9 all-gather.6
